TPU v7x, 256 devices: a whole 4x4x8 slice. The times are simulated.
256 devices in a mesh: wide: 32 (over x, z_lo, y), narrow: 8 (over z_hi, core).
Axes of the slice: x: 4, y: 4, z: 8 (z_hi: 4, z_lo: 2; z = z_hi * 2 + z_lo), core: 2. Of those that a mesh axis runs over, the one named last changes fastest.
Arguments:
- state: float32 [2, 33554432], P(None, ('wide', 'narrow')), may hold values from -6 to 6
- gates: float32 [3, 2, 2, 32, 32], replicated, may hold values from -0.75 to 0.75
- wide_gates: float32 [3, 2, 2, 32, 32], replicated, may hold values from -0.75 to 0.75
- angles: float32 [3, 8], replicated, may hold values from -3.140625 to 3.140625
- coupled: int32 [3, 8], replicated, may hold values from 0 to 16
- sliced_index: int32 [3, 8], replicated, may hold values from 0 to 13
- sliced_values: int32 [14], replicated, may hold values from 0 to 1
Outputs:
- evolved: float32 [2, 33554432], P(None, ('wide', 'narrow'))
All inputs are finite; a program needn't handle non-finite values.
Results may differ from a plain program's by a relative error of at most 0.00018.
Values sent between devices are 32-bit elements; how exact they have to be, the bound alone decides.
A program may use at most 128 MiB of HBM per device.

v0:
```python
import jax
import jax.numpy as jnp
from jax import lax
from jax.sharding import PartitionSpec as P

HIGHEST = lax.Precision.HIGHEST


def from_partner(block, axis, stride):
    count = lax.axis_size(axis)
    route = []
    for low in range(count):
        high = low | 1 << stride
        if high != low and high < count:
            route += [(low, high), (high, low)]
    return lax.ppermute(block, axis, route)


def complex_apply(matrix, amplitudes, form):

    def product(left, right):
        return jnp.einsum(form, left, right, precision=HIGHEST)

    real_part = product(matrix[0], amplitudes[0]) - product(matrix[1], amplitudes[1])
    imag_part = product(matrix[0], amplitudes[1]) + product(matrix[1], amplitudes[0])
    return jnp.stack([real_part, imag_part])


def coupling_table(sliced_index, sliced_values):
    names = jnp.arange(sliced_values.shape[0], dtype=jnp.int32)
    picked = (sliced_index[..., None] == names).astype(jnp.int32) * sliced_values
    return jnp.sum(picked, axis=-1)


def apply_phase(amplitudes, logical, angle_row, coupled_row, value_row):
    phases = jnp.zeros(logical.shape, jnp.float32)
    for coupling in range(angle_row.shape[0]):
        chosen = jnp.right_shift(logical, coupled_row[coupling]) & 1
        phases = phases + angle_row[coupling] * (chosen * value_row[coupling]).astype(jnp.float32)
    cosine = jnp.cos(phases)
    sine_part = jnp.sin(phases)
    return jnp.stack(
        [
            amplitudes[0] * cosine - amplitudes[1] * sine_part,
            amplitudes[0] * sine_part + amplitudes[1] * cosine,
        ]
    )


def remap(amplitudes, narrow_count):
    total = amplitudes.shape[1]
    blocks = amplitudes.reshape(2, narrow_count, total // narrow_count)
    moved = lax.all_to_all(blocks, "narrow", split_axis=1, concat_axis=1, tiled=True)
    return moved.reshape(2, total)


def top_gate(amplitudes, matrix):
    total = amplitudes.shape[1]
    shaped = amplitudes.reshape(2, 32, total // 32)
    return complex_apply(matrix, shaped, "ij,jb->ib").reshape(2, total)


def middle_gate(amplitudes, matrix):
    total = amplitudes.shape[1]
    shaped = amplitudes.reshape(2, 32, 32, total // 1024)
    return complex_apply(matrix, shaped, "ij,ajb->aib").reshape(2, total)


def wide_gate(amplitudes, matrix, wide_bit):
    total = amplitudes.shape[1]
    lowest = total // 1024
    parity = jnp.right_shift(lax.axis_index("wide"), wide_bit) & 1
    rolled = jnp.where(parity == 0, matrix, jnp.roll(matrix, 16, axis=(1, 2)))
    partner = from_partner(amplitudes, "wide", wide_bit)
    paired = jnp.concatenate(
        [amplitudes.reshape(2, 64, 16, lowest), partner.reshape(2, 64, 16, lowest)], axis=2
    )
    mixed = complex_apply(rolled[:, :16], paired, "ij,ajb->aib")
    return mixed.reshape(2, total)


def on_device(state, gates, wide_gates, angles, coupled, sliced_index, sliced_values):
    narrow_count = lax.axis_size("narrow")
    wide_count = lax.axis_size("wide")
    wide_bits = wide_count.bit_length() - 1
    total = state.shape[1]
    values = coupling_table(sliced_index, sliced_values)
    positions = jnp.arange(total, dtype=jnp.int32)
    amplitudes = state
    for layer_index in range(gates.shape[0]):
        amplitudes = apply_phase(
            amplitudes, positions, angles[layer_index], coupled[layer_index], values[layer_index]
        )
        amplitudes = remap(amplitudes, narrow_count)
        amplitudes = top_gate(amplitudes, gates[layer_index, 0])
        amplitudes = remap(amplitudes, narrow_count)
        amplitudes = middle_gate(amplitudes, gates[layer_index, 1])
        for gate_index in range(2):
            wide_bit = (2 * layer_index + gate_index) % wide_bits
            amplitudes = wide_gate(amplitudes, wide_gates[layer_index, gate_index], wide_bit)
    return amplitudes


def solution(mesh):
    in_specs = (P(None, ("wide", "narrow")), P(), P(), P(), P(), P(), P())
    out_specs = P(None, ("wide", "narrow"))
    return jax.shard_map(
        on_device, mesh=mesh, in_specs=in_specs, out_specs=out_specs, check_vma=False
    )
```

profile of v0, /device:TPU:1, one launch (start us, length us, event | category | flops | bytes accessed | tf_op | source)
XLA Modules:
  0.0 573.0 jit_solution(6156286946665051354)
XLA Ops:
  2.4 2.1 fusion.109
  4.5 1.5 fusion.112
  6.0 2.1 fusion.110
  9.6 38.1 %multiply_subtract_fusion.2 = f32[1,131072]{1,0:T(1,128)S(1)} fusion(f32[2,131072]{1,0:T(2,128)} %param.7, s32[]{:T(128)} %bitcast.23, s32[]{:T(128)} %bitcast.22, f32[]{:T(128)} %bitcast.21, s32[]{:T(128)} %bitcast.20, s32[]{:T(128)} %bitcast.19, f32[]{:T(128)} %bitcast.18, s32[]{:T(128)} %bitcast.17, s32[]{:T(128)} %bitcast.16, f32[]{:T(128)} %bitcast.15, ...), kind=kLoop, calls=%fused_computation.91 | loop fusion | flops 6553600 | bytes 1572960 | tf_op jit(solution)/shard_map/sub | solution.py:44
  47.7 37.1 %multiply_add_fusion.5 = f32[1,131072]{1,0:T(1,128)S(1)} fusion(f32[2,131072]{1,0:T(2,128)S(1)} %copy-done, s32[]{:T(128)} %bitcast.23, s32[]{:T(128)} %bitcast.22, f32[]{:T(128)} %bitcast.21, s32[]{:T(128)} %bitcast.20, s32[]{:T(128)} %bitcast.19, f32[]{:T(128)} %bitcast.18, s32[]{:T(128)} %bitcast.17, s32[]{:T(128)} %bitcast.16, f32[]{:T(128)} %bitcast.15, ...), kind=kLoop, calls=%fused_computation.90 | loop fusion | flops 6553600 | bytes 1572960 | tf_op jit(solution)/shard_map/add | solution.py:45
  85.8 35.6 %all_to_all.30 = f32[2,8,16384]{2,0,1:T(2,128)S(1)} all-to-all(f32[2,8,16384]{2,0,1:T(2,128)S(1)} %pad_maximum_fusion.6), channel_id=1, replica_groups=mesh['wide'=32,'narrow'=8] {'narrow'}, dimensions={1} | all-to-all | bytes 2097152 | tf_op jit(solution)/shard_map/all_to_all | solution.py:53
  121.3 2.7 slice_reduce_fusion.5
  128.0 1.9 pad_maximum_fusion.7
  129.9 7.5 %all-to-all-start.1 = ((f32[2,8,16384]{2,0,1:T(2,128)}), f32[2,8,16384]{2,0,1:T(2,128)S(1)}, u32[]{:S(2)}, u32[]{:S(2)}) async-start(f32[2,8,16384]{2,0,1:T(2,128)} %pad_maximum_fusion.7), calls=%async_computation.1 | async-start | bytes 2097152 | tf_op jit(solution)/shard_map/all_to_all | solution.py:53
  138.6 23.1 %all-to-all-done.1 = f32[2,8,16384]{2,0,1:T(2,128)S(1)} async-done(((f32[2,8,16384]{2,0,1:T(2,128)}), f32[2,8,16384]{2,0,1:T(2,128)S(1)}, u32[]{:S(2)}, u32[]{:S(2)}) %all-to-all-start.1) | async-done | bytes 1048608 | tf_op jit(solution)/shard_map/all_to_all | solution.py:53
  166.0 1.6 collective-permute-start
  173.5 12.5 %collective-permute-done = f32[2,131072]{1,0:T(2,128)S(1)} collective-permute-done((f32[2,131072]{1,0:T(2,128)S(1)}, f32[2,131072]{1,0:T(2,128)S(1)}, u32[]{:S(2)}, u32[]{:S(2)}) %collective-permute-start) | collective-permute-done | bytes 1048608 | tf_op jit(solution)/shard_map/ppermute | solution.py:16
  190.1 3.0 collective-permute-start.1
  196.2 14.4 %collective-permute-done.1 = f32[2,131072]{1,0:T(2,128)S(1)} collective-permute-done((f32[2,131072]{1,0:T(2,128)S(1)}, f32[2,131072]{1,0:T(2,128)S(1)}, u32[]{:S(2)}, u32[]{:S(2)}) %collective-permute-start.1) | collective-permute-done | bytes 1048608 | tf_op jit(solution)/shard_map/ppermute | solution.py:16
  214.9 2.2 fusion.8
  218.2 17.5 %multiply_subtract_fusion.1 = f32[1,8,16384]{2,1,0:T(8,128)S(1)} fusion(f32[1,8,16384]{2,1,0:T(8,128)S(1)} %squeeze.528, f32[1,8,16384]{2,1,0:T(8,128)S(1)} %squeeze.503, s32[]{:T(128)} %bitcast.88, s32[]{:T(128)} %bitcast.87, f32[]{:T(128)} %bitcast.86, s32[]{:T(128)} %bitcast.85, s32[]{:T(128)} %bitcast.84, f32[]{:T(128)} %bitcast.83, s32[]{:T(128)} %bitcast.82, ...), kind=kLoop, calls=%fused_computation.87 | loop fusion | flops 6815744 | bytes 1572960 | tf_op jit(solution)/shard_map/sub | solution.py:44
  235.8 17.5 %multiply_add_fusion.2 = f32[1,8,16384]{2,1,0:T(8,128)S(1)} fusion(f32[1,8,16384]{2,1,0:T(8,128)S(1)} %squeeze.528, f32[1,8,16384]{2,1,0:T(8,128)S(1)} %squeeze.503, s32[]{:T(128)} %bitcast.88, s32[]{:T(128)} %bitcast.87, f32[]{:T(128)} %bitcast.86, s32[]{:T(128)} %bitcast.85, s32[]{:T(128)} %bitcast.84, f32[]{:T(128)} %bitcast.83, s32[]{:T(128)} %bitcast.82, ...), kind=kLoop, calls=%fused_computation.86 | loop fusion | flops 6815744 | bytes 1572960 | tf_op jit(solution)/shard_map/add | solution.py:45
  254.2 39.8 %all_to_all.31 = f32[2,8,16384]{2,0,1:T(2,128)S(1)} all-to-all(f32[2,8,16384]{2,0,1:T(2,128)S(1)} %copy.38), channel_id=1, replica_groups=mesh['wide'=32,'narrow'=8] {'narrow'}, dimensions={1} | all-to-all | bytes 2097152 | tf_op jit(solution)/shard_map/all_to_all | solution.py:53
  294.0 2.7 slice_reduce_fusion.3
  301.5 31.8 %all_to_all.32 = f32[2,8,16384]{2,0,1:T(2,128)S(1)} all-to-all(f32[2,8,16384]{2,0,1:T(2,128)S(1)} %pad_maximum_fusion.11), channel_id=1, replica_groups=mesh['wide'=32,'narrow'=8] {'narrow'}, dimensions={1} | all-to-all | bytes 2097152 | tf_op jit(solution)/shard_map/all_to_all | solution.py:53
  337.6 6.0 %collective-permute-start.2 = (f32[2,131072]{1,0:T(2,128)S(1)}, f32[2,131072]{1,0:T(2,128)S(1)}, u32[]{:S(2)}, u32[]{:S(2)}) collective-permute-start(f32[2,131072]{1,0:T(2,128)S(1)} %pad_maximum_fusion.12), channel_id=1, source_target_pairs={{0,32},{32,0},{8,40},{40,8},{16,48},{48,16},{24,56},{56,24},{64,96... | collective-permute-start | bytes 3145736 | tf_op jit(solution)/shard_map/ppermute | solution.py:16
  343.6 22.9 %collective-permute-done.2 = f32[2,131072]{1,0:T(2,128)S(1)} collective-permute-done((f32[2,131072]{1,0:T(2,128)S(1)}, f32[2,131072]{1,0:T(2,128)S(1)}, u32[]{:S(2)}, u32[]{:S(2)}) %collective-permute-start.2) | collective-permute-done | bytes 1048608 | tf_op jit(solution)/shard_map/ppermute | solution.py:16
  371.1 23.4 %collective-permute-done.3 = f32[2,131072]{1,0:T(2,128)S(1)} collective-permute-done((f32[2,131072]{1,0:T(2,128)S(1)}, f32[2,131072]{1,0:T(2,128)S(1)}, u32[]{:S(2)}, u32[]{:S(2)}) %collective-permute-start.3) | collective-permute-done | bytes 1048608 | tf_op jit(solution)/shard_map/ppermute | solution.py:16
  401.9 17.8 %multiply_subtract_fusion = f32[1,8,16384]{2,1,0:T(8,128)S(1)} fusion(f32[1,8,16384]{2,1,0:T(8,128)S(1)} %squeeze.572, f32[1,8,16384]{2,1,0:T(8,128)S(1)} %squeeze.547, s32[]{:T(128)} %bitcast.152, s32[]{:T(128)} %bitcast.151, f32[]{:T(128)} %bitcast.150, s32[]{:T(128)} %bitcast.149, s32[]{:T(128)} %bitcast.148, f32[]{:T(128)} %bitcast.147, s32[]{:T(128)} %bitcast.146, ...), kind=kLoop, calls=%fused_computation.84 | loop fusion | flops 6815744 | bytes 1572960 | tf_op jit(solution)/shard_map/sub | solution.py:44
  419.7 17.8 %multiply_add_fusion = f32[1,8,16384]{2,1,0:T(8,128)S(1)} fusion(f32[1,8,16384]{2,1,0:T(8,128)S(1)} %squeeze.572, f32[1,8,16384]{2,1,0:T(8,128)S(1)} %squeeze.547, s32[]{:T(128)} %bitcast.152, s32[]{:T(128)} %bitcast.151, f32[]{:T(128)} %bitcast.150, s32[]{:T(128)} %bitcast.149, s32[]{:T(128)} %bitcast.148, f32[]{:T(128)} %bitcast.147, s32[]{:T(128)} %bitcast.146, ...), kind=kLoop, calls=%fused_computation.83 | loop fusion | flops 6815744 | bytes 1572960 | tf_op jit(solution)/shard_map/add | solution.py:45
  438.4 27.4 %all_to_all.33 = f32[2,8,16384]{2,0,1:T(2,128)S(1)} all-to-all(f32[2,8,16384]{2,0,1:T(2,128)S(1)} %copy.41), channel_id=1, replica_groups=mesh['wide'=32,'narrow'=8] {'narrow'}, dimensions={1} | all-to-all | bytes 2097152 | tf_op jit(solution)/shard_map/all_to_all | solution.py:53
  465.7 2.7 slice_reduce_fusion.1
  473.2 37.3 %all_to_all.34 = f32[2,8,16384]{2,0,1:T(2,128)S(1)} all-to-all(f32[2,8,16384]{2,0,1:T(2,128)S(1)} %pad_maximum_fusion.15), channel_id=1, replica_groups=mesh['wide'=32,'narrow'=8] {'narrow'}, dimensions={1} | all-to-all | bytes 2097152 | tf_op jit(solution)/shard_map/all_to_all | solution.py:53
  514.9 2.5 collective-permute-start.4
  517.4 22.8 %collective-permute-done.4 = f32[2,131072]{1,0:T(2,128)S(1)} collective-permute-done((f32[2,131072]{1,0:T(2,128)S(1)}, f32[2,131072]{1,0:T(2,128)S(1)}, u32[]{:S(2)}, u32[]{:S(2)}) %collective-permute-start.4) | collective-permute-done | bytes 1048608 | tf_op jit(solution)/shard_map/ppermute | solution.py:16
  546.0 21.3 %collective-permute-done.5 = f32[2,131072]{1,0:T(2,128)S(1)} collective-permute-done((f32[2,131072]{1,0:T(2,128)S(1)}, f32[2,131072]{1,0:T(2,128)S(1)}, u32[]{:S(2)}, u32[]{:S(2)}) %collective-permute-start.5) | collective-permute-done | bytes 1048608 | tf_op jit(solution)/shard_map/ppermute | solution.py:16
  570.9 1.9 pad_maximum_fusion.18
  (129 shorter events, 73.7 us)
Async XLA Ops:
  0.0 47.7 %copy-start = (f32[2,131072]{1,0:T(2,128)S(1)}, f32[2,131072]{1,0:T(2,128)}, u32[]{:S(2)}) copy-start(f32[2,131072]{1,0:T(2,128)} %param.7) | copy-start | bytes 3145732
  121.3 3.0 copy-start.1
  127.9 9.4 %copy-start.2 = (f32[3,2,2,32,32]{4,3,2,1,0:T(8,128)S(1)}, f32[3,2,2,32,32]{4,3,2,1,0:T(8,128)}, u32[]{:S(2)}) copy-start(f32[3,2,2,32,32]{4,3,2,1,0:T(8,128)} %param.9) | copy-start | bytes 147460
  129.9 31.8 %all-to-all-start.1 = ((f32[2,8,16384]{2,0,1:T(2,128)}), f32[2,8,16384]{2,0,1:T(2,128)S(1)}, u32[]{:S(2)}, u32[]{:S(2)}) async-start(f32[2,8,16384]{2,0,1:T(2,128)} %pad_maximum_fusion.7), calls=%async_computation.1 | async-start | bytes 2097152 | tf_op jit(solution)/shard_map/all_to_all | solution.py:53
  164.5 3.1 copy-start.3
  166.0 20.0 %collective-permute-start = (f32[2,131072]{1,0:T(2,128)S(1)}, f32[2,131072]{1,0:T(2,128)S(1)}, u32[]{:S(2)}, u32[]{:S(2)}) collective-permute-start(f32[2,131072]{1,0:T(2,128)S(1)} %pad_maximum_fusion.8), channel_id=1, source_target_pairs={{0,8},{8,0},{16,24},{24,16},{32,40},{40,32},{48,56},{56,48},{64,72... | collective-permute-start | bytes 3145736 | tf_op jit(solution)/shard_map/ppermute | solution.py:16
  188.5 4.7 copy-start.4
  190.1 20.4 %collective-permute-start.1 = (f32[2,131072]{1,0:T(2,128)S(1)}, f32[2,131072]{1,0:T(2,128)S(1)}, u32[]{:S(2)}, u32[]{:S(2)}) collective-permute-start(f32[2,131072]{1,0:T(2,128)S(1)} %pad_maximum_fusion.9), channel_id=1, source_target_pairs={{0,16},{16,0},{8,24},{24,8},{32,48},{48,32},{40,56},{56,40},{64,80... | collective-permute-start | bytes 3145736 | tf_op jit(solution)/shard_map/ppermute | solution.py:16
  196.2 16.1 %copy-start.9 = (f32[2,32,32]{2,1,0:T(8,128)}, f32[2,32,32]{2,1,0:T(8,128)S(1)}, u32[]{:S(2)}) copy-start(f32[2,32,32]{2,1,0:T(8,128)S(1)} %get-tuple-element.28) | copy-start | bytes 24580
  337.6 28.9 %collective-permute-start.2 = (f32[2,131072]{1,0:T(2,128)S(1)}, f32[2,131072]{1,0:T(2,128)S(1)}, u32[]{:S(2)}, u32[]{:S(2)}) collective-permute-start(f32[2,131072]{1,0:T(2,128)S(1)} %pad_maximum_fusion.12), channel_id=1, source_target_pairs={{0,32},{32,0},{8,40},{40,8},{16,48},{48,16},{24,56},{56,24},{64,96... | collective-permute-start | bytes 3145736 | tf_op jit(solution)/shard_map/ppermute | solution.py:16
  366.5 0.8 copy-start.8
  371.0 23.5 %collective-permute-start.3 = (f32[2,131072]{1,0:T(2,128)S(1)}, f32[2,131072]{1,0:T(2,128)S(1)}, u32[]{:S(2)}, u32[]{:S(2)}) collective-permute-start(f32[2,131072]{1,0:T(2,128)S(1)} %pad_maximum_fusion.13), channel_id=1, source_target_pairs={{0,64},{64,0},{8,72},{72,8},{16,80},{80,16},{24,88},{88,24},{32,96... | collective-permute-start | bytes 3145736 | tf_op jit(solution)/shard_map/ppermute | solution.py:16
  394.5 0.8 copy-start.7
  514.9 25.3 %collective-permute-start.4 = (f32[2,131072]{1,0:T(2,128)S(1)}, f32[2,131072]{1,0:T(2,128)S(1)}, u32[]{:S(2)}, u32[]{:S(2)}) collective-permute-start(f32[2,131072]{1,0:T(2,128)S(1)} %pad_maximum_fusion.16), channel_id=1, source_target_pairs={{0,128},{128,0},{8,136},{136,8},{16,144},{144,16},{24,152},{152,24... | collective-permute-start | bytes 3145736 | tf_op jit(solution)/shard_map/ppermute | solution.py:16
  540.2 0.8 copy-start.6
  544.7 22.7 %collective-permute-start.5 = (f32[2,131072]{1,0:T(2,128)S(1)}, f32[2,131072]{1,0:T(2,128)S(1)}, u32[]{:S(2)}, u32[]{:S(2)}) collective-permute-start(f32[2,131072]{1,0:T(2,128)S(1)} %pad_maximum_fusion.17), channel_id=1, source_target_pairs={{0,8},{8,0},{16,24},{24,16},{32,40},{40,32},{48,56},{56,48},{64,72... | collective-permute-start | bytes 3145736 | tf_op jit(solution)/shard_map/ppermute | solution.py:16
  567.4 0.8 copy-start.5
where the time goes:
time: 581 us; the launch traced here: 573 us
  blocking collectives  172 us (30%)
  other arithmetic  167 us (29%)
  waiting for transfers between devices  140 us (24%)
  local copies, waits for them, and re-layouts  36.7 us (6%)
  matrix products  33.8 us (6%)
  starting transfers between devices  22 us (4%)
    all_to_all x5, blocking collectives, remap(): lax.all_to_all(blocks, 'narrow', split_axis=1, concat_axis=1, tiled=True)  172 us
    ppermute x6, waiting for transfers between devices, from_partner(): return lax.ppermute(block, axis, route)  117 us
    sub x3, other arithmetic, apply_phase(): amplitudes[0] * cosine - amplitudes[1] * sine_part  73.4 us
    add x3, other arithmetic, apply_phase(): amplitudes[0] * sine_part + amplitudes[1] * cosine  72.4 us
    dot_general x48, matrix products, product(): return jnp.einsum(form, left, right, precision=HIGHEST)  33.8 us
    all_to_all x1, waiting for transfers between devices, remap(): lax.all_to_all(blocks, 'narrow', split_axis=1, concat_axis=1, tiled=True)  23.1 us
    ppermute x6, starting transfers between devices, from_partner(): return lax.ppermute(block, axis, route)  14.6 us
  transfers between devices with their start and end apart: 7, of which 7 were waited for; matrix products, arithmetic and copies ran while one was open for 2% of the time, Pallas kernels for 0%

commit v1 on v0

v1 whole, which is shorter than its diff:
```python
import functools

import jax
import jax.numpy as jnp
from jax import lax
from jax.experimental import pallas as pl
from jax.experimental.pallas import tpu as pltpu
from jax.sharding import PartitionSpec as P

HIGHEST = lax.Precision.HIGHEST
MESH = pl.DeviceIdType.MESH
PIECES = 4
LANES = 128
F32 = jnp.float32
BF16 = jnp.bfloat16


def iota(shape, axis):
    return lax.broadcasted_iota(jnp.int32, shape, axis)


def halves(value):
    high = value.astype(BF16)
    return high, (value - high.astype(F32)).astype(BF16)


def thirds(value, axis):
    high = value.astype(BF16)
    rest = value - high.astype(F32)
    middle = rest.astype(BF16)
    return jnp.concatenate([high, middle, (rest - middle.astype(F32)).astype(BF16)], axis=axis)


def dot(left, right):
    return jnp.dot(left, right, preferred_element_type=F32)


def one_hot(wanted, own):
    return jnp.where(wanted == own, 1.0, 0.0).astype(BF16)


def on_lanes(real, imag, taken, given, kept_in, kept_out):
    pair = jnp.concatenate([thirds(real, 0), thirds(imag, 0)], axis=1)
    spread = one_hot(iota((96, 256), 0) % 32, given(iota((96, 256), 1)))
    columns = lax.dot_general(pair, spread, (((0,), (0,)), ((), ())), preferred_element_type=F32)
    to_real = iota((32, 256), 1) % 2 == 0
    from_real, from_imag = columns[:32], columns[32:]
    mixed = jnp.concatenate(
        [jnp.where(to_real, from_real, from_imag), jnp.where(to_real, -from_imag, from_real)], axis=0
    )
    rows = iota((256, 192), 0)
    pick = one_hot(iota((256, 192), 1) % 64, (rows % 2) * 32 + taken(rows))
    full = dot(pick, thirds(mixed, 0))
    return jnp.where(kept_in(iota((256, 256), 0)) == kept_out(iota((256, 256), 1)), full, 0.0)


def middle_index(index):
    return (index // 2) % 32


def middle_kept(index):
    return index // 64


def wide_index(index):
    return (index // 128) * 16 + (index // 2) % 16


def wide_kept(index):
    return (index // 32) % 4


def inner_index(index):
    return ((index // 64) % 2) * 16 + (index // 2) % 16


def inner_kept(index):
    return (index // 128) * 2 + (index // 32) % 2


def kernel(
    state, gates, wide, angles, coupled, chosen, values, out,
    loaded, z_send, z_got, xy_send, xy_got, xy_back, xy_home, z_back, z_home, done,
    first_g, rest_g, top_g,
    load_sem, z_s, z_r, xy_s, xy_r, xyb_s, xyb_r, zb_s, zb_r,
):
    w = lax.axis_index("wide")
    n = lax.axis_index("narrow")
    x, y, low, core = w // 8, w % 4, (w // 4) % 2, n % 2
    z = (n // 2) * 2 + low
    z_slot = low * 8 + n
    z_name = z * 2 + core
    xy_name = x * 4 + y

    def z_peer(step):
        other = (z + step // 2) % 8
        side = (core + step) % 2
        lane = (other // 2) * 2 + side
        return (x * 8 + (other % 2) * 4 + y, lane), other * 2 + side, (other % 2) * 8 + lane

    def xy_peer(step):
        across, along = (x + step // 4) % 4, (y + step) % 4
        return (across * 8 + low * 4 + along, n), across * 4 + along

    barrier = pltpu.get_barrier_semaphore()

    @pl.loop(1, 16)
    def _(step):
        pl.semaphore_signal(barrier, inc=1, device_id=z_peer(step)[0], device_id_type=MESH)
        pl.semaphore_signal(barrier, inc=1, device_id=xy_peer(step)[0], device_id_type=MESH)

    load = pltpu.make_async_copy(state, loaded, load_sem)
    load.start()
    load.wait()

    @pl.loop(0, 16)
    def _(block):
        turned = loaded[pl.ds(pl.multiple_of(block * 128, 128), 128), :].T
        for piece in range(PIECES):
            for side in range(2):
                rows = ((block // 2) * 2 + side) * 32 + (block % 2) * 16
                first = piece * 32 + side * 16
                z_send[piece, pl.ds(pl.multiple_of(rows, 16), 16), :] = turned[first : first + 16]

    def slot(index):
        return pl.ds(pl.multiple_of(index * 32, 32), 32)

    pl.semaphore_wait(barrier, 30)

    for piece in range(PIECES):
        @pl.loop(1, 16)
        def _(step):
            device, name, _ = z_peer(step)
            pltpu.make_async_remote_copy(
                src_ref=z_send.at[piece, slot(name)],
                dst_ref=z_got.at[piece, slot(z_slot)],
                send_sem=z_s.at[piece],
                recv_sem=z_r.at[piece],
                device_id=device,
                device_id_type=MESH,
            ).start()

        z_got[piece, slot(z_slot), :] = z_send[piece, slot(z_name), :]

    def arrived(buffer, semaphore, piece):
        part = buffer.at[piece, pl.ds(0, 480)]
        pltpu.make_async_copy(part, part, semaphore.at[piece]).wait()

    row, lane = iota((8, 128), 0), iota((8, 128), 1)
    unmixed = z * 16384 + core * 16 + xy_name
    place = jnp.where(
        row < 3, (lane % 32) * 128, jnp.where(row < 6, (lane % 4) * 4096, unmixed + (lane % 4) * 32)
    )
    phases = jnp.zeros((8, 128), F32)
    for layer in range(3):
        for coupling in range(8):
            turn = angles[layer, coupling] * values[chosen[layer, coupling]].astype(F32)
            bit = jnp.right_shift(place, coupled[layer, coupling]) & 1
            counted = jnp.where((row == layer) | (row == layer + 3) | (row == 6), bit, 0)
            phases = phases + turn * counted.astype(F32)
    cosine, sine = jnp.cos(phases), jnp.sin(phases)

    def turned_gate(gate, layer, phase_row):
        real, imag = gate[layer, 0], gate[layer, 1]
        c = cosine[phase_row : phase_row + 1, :32]
        s = sine[phase_row : phase_row + 1, :32]
        return real * c - imag * s, real * s + imag * c

    for layer in range(3):
        real, imag = turned_gate(gates.at[:, 1], layer, layer)
        middle = on_lanes(real, imag, middle_index, middle_index, middle_kept, middle_kept)
        real, imag = wide[layer, 0, 0], wide[layer, 0, 1]
        if layer == 0:
            plain = on_lanes(real, imag, wide_index, inner_index, wide_kept, inner_kept)
            times_i = on_lanes(-imag, real, wide_index, inner_index, wide_kept, inner_kept)
            first = jnp.dot(middle, jnp.concatenate([plain, times_i], axis=1), precision=HIGHEST, preferred_element_type=F32)
            first_g[0], first_g[1] = halves(first)
        else:
            plain = on_lanes(real, imag, wide_index, wide_index, wide_kept, wide_kept)
            both = jnp.dot(middle, plain, precision=HIGHEST, preferred_element_type=F32)
            rest_g[2 * layer - 1, 0], rest_g[2 * layer - 1, 1] = halves(both)
        real, imag = wide[layer, 1, 0], wide[layer, 1, 1]
        if layer < 2:
            second = on_lanes(real, imag, wide_index, wide_index, wide_kept, wide_kept)
        else:
            second = on_lanes(real, imag, inner_index, wide_index, inner_kept, wide_kept)
        rest_g[2 * layer, 0], rest_g[2 * layer, 1] = halves(second)

    top = [turned_gate(gates.at[:, 0], layer, layer + 3) for layer in range(3)]
    product = jnp.concatenate(top[0], axis=0)
    for real, imag in top[1:]:
        whole = jnp.concatenate(
            [jnp.concatenate([real, -imag], axis=1), jnp.concatenate([imag, real], axis=1)], axis=0
        )
        product = jnp.dot(whole, product, precision=HIGHEST, preferred_element_type=F32)

    def top_index(index):
        return (index % 8) * 4 + ((index // 8) % 2) * 2 + (index // 16) % 2

    def on_rows(real, imag):
        pick = one_hot(iota((128, 96), 1) % 32, top_index(iota((128, 96), 0)))
        part = dot(pick, thirds(jnp.concatenate([real, imag], axis=1), 0))
        columns = iota((192, 256), 1)
        spread = one_hot(iota((192, 256), 0) % 64, ((columns // 32) % 2) * 32 + top_index(columns))
        full = dot(thirds(part, 1), spread)
        return jnp.where(iota((128, 256), 0) // 32 == iota((128, 256), 1) // 64, full, 0.0)

    top_plain = on_rows(product[:32], product[32:])
    top_times_i = on_rows(-product[32:], product[:32])
    for piece in range(PIECES):
        here = (row == 6) & (lane == piece)
        c = jnp.sum(jnp.where(here, cosine, 0.0))
        s = jnp.sum(jnp.where(here, sine, 0.0))
        top_g[piece, 0], top_g[piece, 1] = halves(c * top_plain + s * top_times_i)

    def regroup(source, target, piece):
        for outer in range(16):
            for half in range(2):
                target[piece, pl.ds(outer * 32 + half * 16, 16), :] = source[
                    piece, pl.ds(half * 16 + outer, 16, stride=32), :
                ]

    def send_xy(source, target, sent, got, piece):
        @pl.loop(1, 16)
        def _(step):
            device, name = xy_peer(step)
            pltpu.make_async_remote_copy(
                src_ref=source.at[piece, slot(name)],
                dst_ref=target.at[piece, slot(xy_name)],
                send_sem=sent.at[piece],
                recv_sem=got.at[piece],
                device_id=device,
                device_id_type=MESH,
            ).start()

        target[piece, slot(xy_name), :] = source[piece, slot(xy_name), :]

    def inward(piece):
        arrived(z_got, z_r, piece)
        regroup(z_got, xy_send, piece)
        send_xy(xy_send, xy_got, xy_s, xy_r, piece)

    def right(tiles, zeros, ones, high, low_part):
        both = jnp.concatenate(
            [jnp.concatenate([tiles[k] for k in zeros], axis=0), jnp.concatenate([tiles[k] for k in ones], axis=0)], axis=1
        )
        upper, lower = halves(both)
        return dot(upper, high) + (dot(lower, high) + dot(upper, low_part))

    def gates_on(piece):
        arrived(xy_got, xy_r, piece)
        tiles = [xy_got[piece, pl.ds(k * 8, 8), :] for k in range(64)]
        zeros = [k for k in range(64) if not k & 4]
        mixed = right(tiles, zeros, [k | 4 for k in zeros], first_g[0], first_g[1])
        found = {}
        for place, k in enumerate(zeros):
            for column in range(4):
                found[k, column] = mixed[place * 8 : place * 8 + 8, column * 128 : column * 128 + 128]
        tiles = [None] * 64
        groups = [k for k in range(64) if not k & 6]
        for start in (0, 8):
            columns = []
            for half in range(2):
                columns.append(
                    jnp.concatenate(
                        [
                            found[k | bit13 * 2, times_i * 2 + bit12]
                            for k in groups[start + 4 * half : start + 4 * half + 4]
                            for times_i in range(2)
                            for bit12 in range(2)
                            for bit13 in range(2)
                        ],
                        axis=0,
                    )
                )
            upper, lower = halves(jnp.concatenate(columns, axis=1))
            high, low_part = top_g[piece, 0], top_g[piece, 1]
            topped = dot(high, upper) + (dot(low_part, upper) + dot(high, lower))
            for half in range(2):
                for which, k in enumerate(groups[start + 4 * half : start + 4 * half + 4]):
                    for bit12 in range(2):
                        for bit13 in range(2):
                            at = which * 32 + bit12 * 16 + bit13 * 8
                            tiles[k | bit12 * 4 | bit13 * 2] = topped[at : at + 8, half * 128 : half * 128 + 128]
        for gate, mask in enumerate((8, 1, 16, 32, 4)):
            zeros = [k for k in range(64) if not k & mask]
            mixed = right(tiles, zeros, [k | mask for k in zeros], rest_g[gate, 0], rest_g[gate, 1])
            for place, k in enumerate(zeros):
                tiles[k] = mixed[place * 8 : place * 8 + 8, :128]
                tiles[k | mask] = mixed[place * 8 : place * 8 + 8, 128:]
        for k in range(64):
            xy_back[piece, pl.ds(k * 8, 8), :] = tiles[k]
        send_xy(xy_back, xy_home, xyb_s, xyb_r, piece)

    def outward(piece):
        arrived(xy_home, xyb_r, piece)
        regroup(xy_home, z_back, piece)

        @pl.loop(1, 16)
        def _(step):
            device, _, there = z_peer(step)
            pltpu.make_async_remote_copy(
                src_ref=z_back.at[piece, slot(there)],
                dst_ref=z_home.at[piece, slot(z_name)],
                send_sem=zb_s.at[piece],
                recv_sem=zb_r.at[piece],
                device_id=device,
                device_id_type=MESH,
            ).start()

        z_home[piece, slot(z_name), :] = z_back[piece, slot(z_slot), :]

    @pl.loop(0, PIECES + 2)
    def _(step):
        @pl.when(step < PIECES)
        def _():
            inward(step)

        @pl.when((step >= 1) & (step < PIECES + 1))
        def _():
            gates_on(step - 1)

        @pl.when(step >= 2)
        def _():
            outward(step - 2)

    for piece in range(PIECES):
        arrived(z_home, zb_r, piece)

    @pl.loop(0, 16)
    def _(block):
        parts = []
        for piece in range(PIECES):
            for side in range(2):
                rows = ((block // 2) * 2 + side) * 32 + (block % 2) * 16
                parts.append(z_home[piece, pl.ds(pl.multiple_of(rows, 16), 16), :])
        done[pl.ds(pl.multiple_of(block * 128, 128), 128), :] = jnp.concatenate(parts, axis=0).T

    store = pltpu.make_async_copy(done, out, load_sem)
    store.start()
    for piece in range(PIECES):
        arrived(z_send, z_s, piece)
        arrived(xy_send, xy_s, piece)
        arrived(xy_back, xyb_s, piece)
        arrived(z_back, zb_s, piece)
    store.wait()


def on_device(state, gates, wide_gates, angles, coupled, sliced_index, sliced_values):
    rows = state.size // LANES
    linear = state.reshape(2, rows // 2, LANES).transpose(1, 0, 2).reshape(rows, LANES)
    any_space = pl.BlockSpec(memory_space=pl.ANY)
    vmem = pl.BlockSpec(memory_space=pltpu.VMEM)
    smem = pl.BlockSpec(memory_space=pltpu.SMEM)
    whole = pltpu.VMEM((rows, LANES), F32)
    pieces = pltpu.VMEM((PIECES, rows // PIECES, LANES), F32)
    counts = pltpu.SemaphoreType.DMA((PIECES,))
    result = pl.pallas_call(
        kernel,
        out_shape=jax.ShapeDtypeStruct((rows, LANES), F32),
        in_specs=[any_space, vmem, vmem, smem, smem, smem, smem],
        out_specs=any_space,
        scratch_shapes=[
            whole, pieces, pieces, pieces, pieces, pieces, pieces, pieces, pieces, whole,
            pltpu.VMEM((2, 256, 512), BF16),
            pltpu.VMEM((5, 2, 256, 256), BF16),
            pltpu.VMEM((PIECES, 2, 128, 256), BF16),
            pltpu.SemaphoreType.DMA,
            counts, counts, counts, counts, counts, counts, counts, counts,
        ],
        compiler_params=pltpu.CompilerParams(
            collective_id=0, has_side_effects=True, vmem_limit_bytes=40 << 20
        ),
        cost_estimate=pl.CostEstimate(flops=1 << 31, bytes_accessed=1 << 21, transcendentals=0),
    )(linear, gates, wide_gates, angles, coupled, sliced_index, sliced_values)
    return result.reshape(rows // 2, 2, LANES).transpose(1, 0, 2).reshape(state.shape)


def solution(mesh):
    in_specs = (P(None, ("wide", "narrow")), P(), P(), P(), P(), P(), P())
    out_specs = P(None, ("wide", "narrow"))
    return jax.shard_map(
        on_device, mesh=mesh, in_specs=in_specs, out_specs=out_specs, check_vma=False
    )
```

time: 581 us -> 71.8 us (0.12); the launches traced: 573 us -> 71.5 us
  blocking collectives: 172 us -> 0 us
  other arithmetic: 167 us -> 0 us
  waiting for transfers between devices: 140 us -> 0 us
  Pallas kernels: 0 us -> 64.8 us
  matrix products: 33.8 us -> 0 us
  local copies, waits for them, and re-layouts: 36.7 us -> 6.75 us
  starting transfers between devices: 22 us -> 0 us
    all_to_all x5 -> x0, blocking collectives: 172 us -> none  [remap(): lax.all_to_all(blocks, 'narrow', split_axis=1, concat_axis=1, tiled=True)]
    ppermute x6 -> x0, waiting for transfers between devices: 117 us -> none  [from_partner(): return lax.ppermute(block, axis, route)]
    sub x3 -> x0, other arithmetic: 73.4 us -> none  [apply_phase(): amplitudes[0] * cosine - amplitudes[1] * sine_part]
    add x3 -> x0, other arithmetic: 72.4 us -> none  [apply_phase(): amplitudes[0] * sine_part + amplitudes[1] * cosine]
    pallas_call x0 -> x1, Pallas kernels: none -> 64.8 us  [on_device(): pl.pallas_call(kernel, out_shape=jax.ShapeDtypeStruct((rows, LANES), F32)...]
    dot_general x48 -> x0, matrix products: 33.8 us -> none  [product(): return jnp.einsum(form, left, right, precision=HIGHEST)]
    all_to_all x1 -> x0, waiting for transfers between devices: 23.1 us -> none  [remap(): lax.all_to_all(blocks, 'narrow', split_axis=1, concat_axis=1, tiled=True)]
    slice x15 -> x0, local copies, waits for them, and re-layouts: 23.1 us -> none  [the longest x6 11.1 us: complex_apply(): amplitudes[0]]
  transfers between devices with their start and end apart: 7 -> 0, of which waited for: 7 -> 0; matrix products, arithmetic and copies ran while one was open for 2% -> 0% of each run, Pallas kernels for 0% -> 0%
where the time goes in v1:
time: 71.8 us; the launch traced here: 71.5 us
  Pallas kernels  64.8 us (90%)
  local copies, waits for them, and re-layouts  6.75 us (9%)
    pallas_call x1, Pallas kernels, on_device(): pl.pallas_call(kernel, out_shape=jax.ShapeDtypeStruct((rows, LANES), F32)...  64.8 us
    unnamed x15, local copies, waits for them, and re-layouts  6.75 us

profile of v1, /device:TPU:1, one launch (start us, length us, event | category | flops | bytes accessed | tf_op | source)
XLA Modules:
  0.0 71.5 jit_solution(2039972406419536241)
XLA Ops:
  0.0 0.0 copy-start.6
  0.0 0.7 copy-done.6
  0.7 0.0 copy-start
  0.7 1.2 %copy-done = f32[2,131072]{1,0:T(2,128)S(1)} copy-done((f32[2,131072]{1,0:T(2,128)S(1)}, f32[2,131072]{1,0:T(2,128)}, u32[]{:S(2)}) %copy-start) | copy-done | bytes 1048600
  1.9 0.0 copy-start.1
  1.9 0.9 %copy-done.1 = f32[3,2,2,32,32]{4,3,2,1,0:T(8,128)S(1)} copy-done((f32[3,2,2,32,32]{4,3,2,1,0:T(8,128)S(1)}, f32[3,2,2,32,32]{4,3,2,1,0:T(8,128)}, u32[]{:S(2)}) %copy-start.1) | copy-done | bytes 49176
  2.8 0.0 copy-start.2
  2.8 0.9 %copy-done.2 = f32[3,2,2,32,32]{4,3,2,1,0:T(8,128)S(1)} copy-done((f32[3,2,2,32,32]{4,3,2,1,0:T(8,128)S(1)}, f32[3,2,2,32,32]{4,3,2,1,0:T(8,128)}, u32[]{:S(2)}) %copy-start.2) | copy-done | bytes 49176
  3.7 0.0 copy-start.3
  3.7 0.7 copy-done.3
  4.4 0.0 copy-start.4
  4.4 0.7 copy-done.4
  5.1 0.0 copy-start.5
  5.1 0.7 copy-done.5
  5.8 64.8 %shard_map.73 = f32[2048,128]{1,0:T(8,128)S(1)} custom-call(f32[2048,128]{1,0:T(8,128)S(1)} %bitcast.11, f32[3,2,2,32,32]{4,3,2,1,0:T(8,128)S(1)} %copy-done.1, f32[3,2,2,32,32]{4,3,2,1,0:T(8,128)S(1)} %copy-done.2, f32[3,8]{1,0:T(4,128)S(1)} %copy-done.3, s32[3,8]{1,0:T(4,128)S(1)} %copy-done.4, s32[3,8]{1,0:T(4,128)S(1)} %copy-done.5, s32[14]{0:T(128)S(1)} %copy-done.6), custom_call_target="tpu_custom_call" | custom-call | flops 2147483648 | bytes 2097152 | tf_op jit(solution)/shard_map/pallas_call | solution.py:358
  70.6 1.0 %copy.11 = f32[2,131072]{1,0:T(2,128)} copy(f32[2,131072]{1,0:T(2,128)S(1)} %bitcast.10) | data formatting | bytes 2097152
Async XLA Ops:
  0.0 0.7 copy-start.6
  0.7 1.2 %copy-start = (f32[2,131072]{1,0:T(2,128)S(1)}, f32[2,131072]{1,0:T(2,128)}, u32[]{:S(2)}) copy-start(f32[2,131072]{1,0:T(2,128)} %param.7) | copy-start | bytes 3145732
  1.9 0.9 %copy-start.1 = (f32[3,2,2,32,32]{4,3,2,1,0:T(8,128)S(1)}, f32[3,2,2,32,32]{4,3,2,1,0:T(8,128)}, u32[]{:S(2)}) copy-start(f32[3,2,2,32,32]{4,3,2,1,0:T(8,128)} %gates.1) | copy-start | bytes 147460
  2.8 0.9 %copy-start.2 = (f32[3,2,2,32,32]{4,3,2,1,0:T(8,128)S(1)}, f32[3,2,2,32,32]{4,3,2,1,0:T(8,128)}, u32[]{:S(2)}) copy-start(f32[3,2,2,32,32]{4,3,2,1,0:T(8,128)} %wide.1) | copy-start | bytes 147460
  3.7 0.7 copy-start.3
  4.4 0.7 copy-start.4
  5.1 0.7 copy-start.5

commit v2 on v1

--- a/solution.py
+++ b/solution.py
@@ -10,6 +10,7 @@
 HIGHEST = lax.Precision.HIGHEST
 MESH = pl.DeviceIdType.MESH
 PIECES = 4
+EARLY = 2
 LANES = 128
 F32 = jnp.float32
 BF16 = jnp.bfloat16
@@ -79,10 +80,11 @@
 
 
 def kernel(
-    state, gates, wide, angles, coupled, chosen, values, out,
-    loaded, z_send, z_got, xy_send, xy_got, xy_back, xy_home, z_back, z_home, done,
+    state, gates_in, wide_in, angles_in, coupled_in, chosen_in, values_in, out,
+    gates, wide, angles, coupled, chosen, values,
+    loaded, z_send, z_got, xy_send, early, ready, mixed, late, xy_home, z_back, z_home,
     first_g, rest_g, top_g,
-    load_sem, z_s, z_r, xy_s, xy_r, xyb_s, xyb_r, zb_s, zb_r,
+    load_sem, small_sems, z_s, z_r, xy_s, xy_r, xyb_s, xyb_r, zb_s, zb_r,
 ):
     w = lax.axis_index("wide")
     n = lax.axis_index("narrow")
@@ -111,41 +113,87 @@
 
     load = pltpu.make_async_copy(state, loaded, load_sem)
     load.start()
+    small = [
+        pltpu.make_async_copy(source, target, small_sems.at[place])
+        for place, (source, target) in enumerate(
+            [
+                (gates_in, gates), (wide_in, wide), (angles_in, angles),
+                (coupled_in, coupled), (chosen_in, chosen), (values_in, values),
+            ]
+        )
+    ]
+    for copy in small:
+        copy.start()
     load.wait()
 
-    @pl.loop(0, 16)
+    @pl.loop(0, 16, unroll=16)
     def _(block):
         turned = loaded[pl.ds(pl.multiple_of(block * 128, 128), 128), :].T
         for piece in range(PIECES):
             for side in range(2):
-                rows = ((block // 2) * 2 + side) * 32 + (block % 2) * 16
+                name, half = (block // 2) * 2 + side, (block % 2) * 16
                 first = piece * 32 + side * 16
-                z_send[piece, pl.ds(pl.multiple_of(rows, 16), 16), :] = turned[first : first + 16]
+                if piece == EARLY:
+                    rows = pl.ds(half + name, 16, stride=32)
+                    xy_send[piece, rows, :] = turned[first : first + 16]
+                else:
+                    rows = pl.ds(pl.multiple_of(name * 32 + half, 16), 16)
+                    z_send[piece, rows, :] = turned[first : first + 16]
 
     def slot(index):
         return pl.ds(pl.multiple_of(index * 32, 32), 32)
 
     pl.semaphore_wait(barrier, 30)
 
-    for piece in range(PIECES):
+    def send_z(source, target, sent, got, piece, inward):
         @pl.loop(1, 16)
         def _(step):
-            device, name, _ = z_peer(step)
+            device, name, there = z_peer(step)
             pltpu.make_async_remote_copy(
-                src_ref=z_send.at[piece, slot(name)],
-                dst_ref=z_got.at[piece, slot(z_slot)],
-                send_sem=z_s.at[piece],
-                recv_sem=z_r.at[piece],
+                src_ref=source.at[piece, slot(name if inward else there)],
+                dst_ref=target.at[piece, slot(z_slot if inward else z_name)],
+                send_sem=sent.at[piece],
+                recv_sem=got.at[piece],
                 device_id=device,
                 device_id_type=MESH,
             ).start()
 
-        z_got[piece, slot(z_slot), :] = z_send[piece, slot(z_name), :]
+        own, landing = (z_name, z_slot) if inward else (z_slot, z_name)
+        target[piece, slot(landing), :] = source[piece, slot(own), :]
+
+    def send_xy(source, at, target, to, sent, got, piece):
+        @pl.loop(1, 16)
+        def _(step):
+            device, name = xy_peer(step)
+            pltpu.make_async_remote_copy(
+                src_ref=source.at[at, slot(name)],
+                dst_ref=target.at[to, slot(xy_name)],
+                send_sem=sent.at[piece],
+                recv_sem=got.at[piece],
+                device_id=device,
+                device_id_type=MESH,
+            ).start()
+
+        target[to, slot(xy_name), :] = source[at, slot(xy_name), :]
 
     def arrived(buffer, semaphore, piece):
-        part = buffer.at[piece, pl.ds(0, 480)]
+        part = buffer.at[0, pl.ds(0, 480)]
         pltpu.make_async_copy(part, part, semaphore.at[piece]).wait()
 
+    def regroup(source, at, target, to):
+        for outer in range(16):
+            for half in range(2):
+                target[to, pl.ds(outer * 32 + half * 16, 16), :] = source[
+                    at, pl.ds(half * 16 + outer, 16, stride=32), :
+                ]
+
+    send_z(z_send, z_got, z_s, z_r, 0, True)
+    send_xy(xy_send, EARLY, early, 0, xy_s, xy_r, EARLY)
+    send_z(z_send, z_got, z_s, z_r, 1, True)
+    send_z(z_send, z_got, z_s, z_r, 3, True)
+
+    for copy in small:
+        copy.wait()
     row, lane = iota((8, 128), 0), iota((8, 128), 1)
     unmixed = z * 16384 + core * 16 + xy_name
     place = jnp.where(
@@ -213,33 +261,6 @@
         s = jnp.sum(jnp.where(here, sine, 0.0))
         top_g[piece, 0], top_g[piece, 1] = halves(c * top_plain + s * top_times_i)
 
-    def regroup(source, target, piece):
-        for outer in range(16):
-            for half in range(2):
-                target[piece, pl.ds(outer * 32 + half * 16, 16), :] = source[
-                    piece, pl.ds(half * 16 + outer, 16, stride=32), :
-                ]
-
-    def send_xy(source, target, sent, got, piece):
-        @pl.loop(1, 16)
-        def _(step):
-            device, name = xy_peer(step)
-            pltpu.make_async_remote_copy(
-                src_ref=source.at[piece, slot(name)],
-                dst_ref=target.at[piece, slot(xy_name)],
-                send_sem=sent.at[piece],
-                recv_sem=got.at[piece],
-                device_id=device,
-                device_id_type=MESH,
-            ).start()
-
-        target[piece, slot(xy_name), :] = source[piece, slot(xy_name), :]
-
-    def inward(piece):
-        arrived(z_got, z_r, piece)
-        regroup(z_got, xy_send, piece)
-        send_xy(xy_send, xy_got, xy_s, xy_r, piece)
-
     def right(tiles, zeros, ones, high, low_part):
         both = jnp.concatenate(
             [jnp.concatenate([tiles[k] for k in zeros], axis=0), jnp.concatenate([tiles[k] for k in ones], axis=0)], axis=1
@@ -248,14 +269,13 @@
         return dot(upper, high) + (dot(lower, high) + dot(upper, low_part))
 
     def gates_on(piece):
-        arrived(xy_got, xy_r, piece)
-        tiles = [xy_got[piece, pl.ds(k * 8, 8), :] for k in range(64)]
+        tiles = [ready[piece, pl.ds(k * 8, 8), :] for k in range(64)]
         zeros = [k for k in range(64) if not k & 4]
-        mixed = right(tiles, zeros, [k | 4 for k in zeros], first_g[0], first_g[1])
+        product = right(tiles, zeros, [k | 4 for k in zeros], first_g[0], first_g[1])
         found = {}
         for place, k in enumerate(zeros):
             for column in range(4):
-                found[k, column] = mixed[place * 8 : place * 8 + 8, column * 128 : column * 128 + 128]
+                found[k, column] = product[place * 8 : place * 8 + 8, column * 128 : column * 128 + 128]
         tiles = [None] * 64
         groups = [k for k in range(64) if not k & 6]
         for start in (0, 8):
@@ -284,95 +304,130 @@
                             tiles[k | bit12 * 4 | bit13 * 2] = topped[at : at + 8, half * 128 : half * 128 + 128]
         for gate, mask in enumerate((8, 1, 16, 32, 4)):
             zeros = [k for k in range(64) if not k & mask]
-            mixed = right(tiles, zeros, [k | mask for k in zeros], rest_g[gate, 0], rest_g[gate, 1])
+            product = right(tiles, zeros, [k | mask for k in zeros], rest_g[gate, 0], rest_g[gate, 1])
             for place, k in enumerate(zeros):
-                tiles[k] = mixed[place * 8 : place * 8 + 8, :128]
-                tiles[k | mask] = mixed[place * 8 : place * 8 + 8, 128:]
+                tiles[k] = product[place * 8 : place * 8 + 8, :128]
+                tiles[k | mask] = product[place * 8 : place * 8 + 8, 128:]
         for k in range(64):
-            xy_back[piece, pl.ds(k * 8, 8), :] = tiles[k]
-        send_xy(xy_back, xy_home, xyb_s, xyb_r, piece)
-
-    def outward(piece):
+            mixed[piece, pl.ds(k * 8, 8), :] = tiles[k]
+
+    def inward(piece):
+        arrived(z_got, z_r, piece)
+        regroup(z_got, piece, xy_send, piece)
+        send_xy(xy_send, piece, ready, piece, xy_s, xy_r, piece)
+
+    arrived(early, xy_r, EARLY)
+    regroup(early, 0, z_send, EARLY)
+    send_z(z_send, z_got, z_s, z_r, EARLY, True)
+
+    @pl.loop(0, 2)
+    def _(piece):
+        inward(piece)
+
+    @pl.loop(0, PIECES)
+    def _(piece):
+        @pl.when(piece == 1)
+        def _():
+            inward(3)
+
+        @pl.when(piece == EARLY)
+        def _():
+            arrived(z_got, z_r, EARLY)
+            regroup(z_got, EARLY, ready, EARLY)
+
+        @pl.when(piece != EARLY)
+        def _():
+            arrived(ready, xy_r, piece)
+
+        gates_on(piece)
+
+        @pl.when(piece < 2)
+        def _():
+            regroup(mixed, piece, z_back, piece)
+            send_z(z_back, z_home, zb_s, zb_r, piece, False)
+
+        @pl.when(piece >= 2)
+        def _():
+            send_xy(mixed, piece, xy_home, piece, xyb_s, xyb_r, piece)
+
+    def finish_late(piece):
+        arrived(z_home, zb_r, piece)
+        regroup(z_home, piece, late, piece)
+        send_xy(late, piece, xy_home, piece, xyb_s, xyb_r, piece)
+
+    finish_late(0)
+
+    @pl.loop(2, PIECES)
+    def _(piece):
         arrived(xy_home, xyb_r, piece)
-        regroup(xy_home, z_back, piece)
-
-        @pl.loop(1, 16)
-        def _(step):
-            device, _, there = z_peer(step)
-            pltpu.make_async_remote_copy(
-                src_ref=z_back.at[piece, slot(there)],
-                dst_ref=z_home.at[piece, slot(z_name)],
-                send_sem=zb_s.at[piece],
-                recv_sem=zb_r.at[piece],
-                device_id=device,
-                device_id_type=MESH,
-            ).start()
-
-        z_home[piece, slot(z_name), :] = z_back[piece, slot(z_slot), :]
-
-    @pl.loop(0, PIECES + 2)
-    def _(step):
-        @pl.when(step < PIECES)
-        def _():
-            inward(step)
-
-        @pl.when((step >= 1) & (step < PIECES + 1))
-        def _():
-            gates_on(step - 1)
-
-        @pl.when(step >= 2)
-        def _():
-            outward(step - 2)
-
-    for piece in range(PIECES):
-        arrived(z_home, zb_r, piece)
-
-    @pl.loop(0, 16)
+        regroup(xy_home, piece, z_back, piece)
+        send_z(z_back, z_home, zb_s, zb_r, piece, False)
+
+    finish_late(1)
+    for piece in range(2):
+        arrived(xy_home, xyb_r, piece)
+        arrived(z_home, zb_r, piece + 2)
+
+    @pl.loop(0, 16, unroll=16)
     def _(block):
         parts = []
         for piece in range(PIECES):
             for side in range(2):
-                rows = ((block // 2) * 2 + side) * 32 + (block % 2) * 16
-                parts.append(z_home[piece, pl.ds(pl.multiple_of(rows, 16), 16), :])
-        done[pl.ds(pl.multiple_of(block * 128, 128), 128), :] = jnp.concatenate(parts, axis=0).T
-
-    store = pltpu.make_async_copy(done, out, load_sem)
-    store.start()
+                name, half = (block // 2) * 2 + side, (block % 2) * 16
+                if piece < 2:
+                    parts.append(xy_home[piece, pl.ds(half + name, 16, stride=32), :])
+                else:
+                    parts.append(z_home[piece, pl.ds(pl.multiple_of(name * 32 + half, 16), 16), :])
+        out[pl.ds(pl.multiple_of(block * 128, 128), 128), :] = jnp.concatenate(parts, axis=0).T
+
     for piece in range(PIECES):
         arrived(z_send, z_s, piece)
         arrived(xy_send, xy_s, piece)
-        arrived(xy_back, xyb_s, piece)
+        arrived(mixed, xyb_s, piece)
         arrived(z_back, zb_s, piece)
-    store.wait()
 
 
 def on_device(state, gates, wide_gates, angles, coupled, sliced_index, sliced_values):
     rows = state.size // LANES
     linear = state.reshape(2, rows // 2, LANES).transpose(1, 0, 2).reshape(rows, LANES)
-    any_space = pl.BlockSpec(memory_space=pl.ANY)
-    vmem = pl.BlockSpec(memory_space=pltpu.VMEM)
-    smem = pl.BlockSpec(memory_space=pltpu.SMEM)
+    hbm = pl.BlockSpec(memory_space=pltpu.HBM)
     whole = pltpu.VMEM((rows, LANES), F32)
-    pieces = pltpu.VMEM((PIECES, rows // PIECES, LANES), F32)
+
+    def pieces(count):
+        return pltpu.VMEM((count, rows // PIECES, LANES), F32)
+
     counts = pltpu.SemaphoreType.DMA((PIECES,))
     result = pl.pallas_call(
         kernel,
-        out_shape=jax.ShapeDtypeStruct((rows, LANES), F32),
-        in_specs=[any_space, vmem, vmem, smem, smem, smem, smem],
-        out_specs=any_space,
+        out_shape=pltpu.VMEM((rows, LANES), F32),
+        in_specs=[hbm] * 7,
+        out_specs=pl.BlockSpec(memory_space=pltpu.VMEM),
         scratch_shapes=[
-            whole, pieces, pieces, pieces, pieces, pieces, pieces, pieces, pieces, whole,
+            pltpu.VMEM(gates.shape, F32),
+            pltpu.VMEM(wide_gates.shape, F32),
+            pltpu.SMEM(angles.shape, F32),
+            pltpu.SMEM(coupled.shape, jnp.int32),
+            pltpu.SMEM(sliced_index.shape, jnp.int32),
+            pltpu.SMEM(sliced_values.shape, jnp.int32),
+            whole, pieces(4), pieces(4), pieces(4), pieces(1), pieces(4), pieces(4), pieces(2), pieces(4), pieces(4),
+            pieces(4),
             pltpu.VMEM((2, 256, 512), BF16),
             pltpu.VMEM((5, 2, 256, 256), BF16),
             pltpu.VMEM((PIECES, 2, 128, 256), BF16),
             pltpu.SemaphoreType.DMA,
+            pltpu.SemaphoreType.DMA((6,)),
             counts, counts, counts, counts, counts, counts, counts, counts,
         ],
         compiler_params=pltpu.CompilerParams(
-            collective_id=0, has_side_effects=True, vmem_limit_bytes=40 << 20
+            collective_id=0, has_side_effects=True, vmem_limit_bytes=48 << 20
         ),
         cost_estimate=pl.CostEstimate(flops=1 << 31, bytes_accessed=1 << 21, transcendentals=0),
-    )(linear, gates, wide_gates, angles, coupled, sliced_index, sliced_values)
+    )(
+        *(
+            pltpu.with_memory_space_constraint(each, pltpu.HBM)
+            for each in (linear, gates, wide_gates, angles, coupled, sliced_index, sliced_values)
+        )
+    )
     return result.reshape(rows // 2, 2, LANES).transpose(1, 0, 2).reshape(state.shape)
 
 

time: 71.8 us -> 61.5 us (0.86)
  local copies, waits for them, and re-layouts: 6.75 us -> 0.97 us
  Pallas kernels: 64.8 us -> 60.4 us
    unnamed x15 -> x1, local copies, waits for them, and re-layouts: 6.75 us -> 0.97 us
    pallas_call x1, Pallas kernels: 64.8 us -> 60.4 us  [on_device(): pl.pallas_call(kernel, out_shape=pltpu.VMEM((rows, LANES), F32), in_specs...]
where the time goes in v2:
time: 61.5 us; the launch traced here: 61.4 us
  Pallas kernels  60.4 us (98%)
  local copies, waits for them, and re-layouts  0.97 us (2%)
    pallas_call x1, Pallas kernels, on_device(): pl.pallas_call(kernel, out_shape=pltpu.VMEM((rows, LANES), F32), in_specs...  60.4 us

profile of v2, /device:TPU:1, one launch (start us, length us, event | category | flops | bytes accessed | tf_op | source)
XLA Modules:
  0.0 61.4 jit_solution(4748331395509429033)
XLA Ops:
  0.0 60.4 %shard_map.73 = f32[2048,128]{1,0:T(8,128)S(1)} custom-call(f32[2048,128]{1,0:T(8,128)} %bitcast.11, f32[3,2,2,32,32]{4,3,2,1,0:T(8,128)} %gates_in.1, f32[3,2,2,32,32]{4,3,2,1,0:T(8,128)} %wide_in.1, f32[3,8]{1,0:T(4,128)} %angles_in.1, s32[3,8]{1,0:T(4,128)} %coupled_in.1, s32[3,8]{1,0:T(4,128)} %chosen_in.1, s32[14]{0:T(128)} %values_in.1), custom_call_target="tpu_custom_call" | custom-call | flops 2147483648 | bytes 2097152 | tf_op jit(solution)/shard_map/pallas_call | solution.py:400
  60.4 1.0 %copy.11 = f32[2,131072]{1,0:T(2,128)} copy(f32[2,131072]{1,0:T(2,128)S(1)} %bitcast.10) | data formatting | bytes 2097152

commit v3 on v2

--- a/solution.py
+++ b/solution.py
@@ -10,7 +10,6 @@
 HIGHEST = lax.Precision.HIGHEST
 MESH = pl.DeviceIdType.MESH
 PIECES = 4
-EARLY = 2
 LANES = 128
 F32 = jnp.float32
 BF16 = jnp.bfloat16
@@ -82,9 +81,9 @@
 def kernel(
     state, gates_in, wide_in, angles_in, coupled_in, chosen_in, values_in, out,
     gates, wide, angles, coupled, chosen, values,
-    loaded, z_send, z_got, xy_send, early, ready, mixed, late, xy_home, z_back, z_home,
+    loaded, z_send, z_got, xy_send, xy_got, ready, mixed, late, xy_home, z_back, z_home,
     first_g, rest_g, top_g,
-    load_sem, small_sems, z_s, z_r, xy_s, xy_r, xyb_s, xyb_r, zb_s, zb_r,
+    load_sems, small_sems, z_s, z_r, xy_s, xy_r, xyb_s, xyb_r, zb_s, zb_r,
 ):
     w = lax.axis_index("wide")
     n = lax.axis_index("narrow")
@@ -95,8 +94,9 @@
     xy_name = x * 4 + y
 
     def z_peer(step):
-        other = (z + step // 2) % 8
-        side = (core + step) % 2
+        far = (step - 1) % 8
+        other = (z + 4 + (1 - 2 * (far % 2)) * ((far + 1) // 2)) % 8
+        side = (core + 1 + (step - 1) // 8) % 2
         lane = (other // 2) * 2 + side
         return (x * 8 + (other % 2) * 4 + y, lane), other * 2 + side, (other % 2) * 8 + lane
 
@@ -106,13 +106,23 @@
 
     barrier = pltpu.get_barrier_semaphore()
 
+    loads = [
+        pltpu.make_async_copy(
+            state.at[pl.ds(part * 512, 512)], loaded.at[pl.ds(part * 512, 512)], load_sems.at[part]
+        )
+        for part in range(4)
+    ]
+    for load in loads:
+        load.start()
+
     @pl.loop(1, 16)
     def _(step):
         pl.semaphore_signal(barrier, inc=1, device_id=z_peer(step)[0], device_id_type=MESH)
+
+    @pl.loop(1, 16)
+    def _(step):
         pl.semaphore_signal(barrier, inc=1, device_id=xy_peer(step)[0], device_id_type=MESH)
 
-    load = pltpu.make_async_copy(state, loaded, load_sem)
-    load.start()
     small = [
         pltpu.make_async_copy(source, target, small_sems.at[place])
         for place, (source, target) in enumerate(
@@ -124,26 +134,22 @@
     ]
     for copy in small:
         copy.start()
-    load.wait()
-
-    @pl.loop(0, 16, unroll=16)
-    def _(block):
-        turned = loaded[pl.ds(pl.multiple_of(block * 128, 128), 128), :].T
-        for piece in range(PIECES):
-            for side in range(2):
-                name, half = (block // 2) * 2 + side, (block % 2) * 16
-                first = piece * 32 + side * 16
-                if piece == EARLY:
-                    rows = pl.ds(half + name, 16, stride=32)
-                    xy_send[piece, rows, :] = turned[first : first + 16]
+    def turn(piece):
+        loads[piece].wait()
+        for block in range(4):
+            start = piece * 512 + block * 128
+            turned = loaded[start : start + 128, :].T
+            for part in range(8):
+                name, half = (block // 2) * 8 + part, (block % 2) * 16
+                rows = turned[part * 16 : part * 16 + 16]
+                if piece % 2:
+                    xy_send[piece, pl.ds(half + name, 16, stride=32), :] = rows
                 else:
-                    rows = pl.ds(pl.multiple_of(name * 32 + half, 16), 16)
-                    z_send[piece, rows, :] = turned[first : first + 16]
+                    z_send[piece, pl.ds(name * 32 + half, 16), :] = rows
 
     def slot(index):
         return pl.ds(pl.multiple_of(index * 32, 32), 32)
 
-    pl.semaphore_wait(barrier, 30)
 
     def send_z(source, target, sent, got, piece, inward):
         @pl.loop(1, 16)
@@ -161,43 +167,47 @@
         own, landing = (z_name, z_slot) if inward else (z_slot, z_name)
         target[piece, slot(landing), :] = source[piece, slot(own), :]
 
-    def send_xy(source, at, target, to, sent, got, piece):
+    def send_xy(source, target, sent, got, piece):
         @pl.loop(1, 16)
         def _(step):
             device, name = xy_peer(step)
             pltpu.make_async_remote_copy(
-                src_ref=source.at[at, slot(name)],
-                dst_ref=target.at[to, slot(xy_name)],
+                src_ref=source.at[piece, slot(name)],
+                dst_ref=target.at[piece, slot(xy_name)],
                 send_sem=sent.at[piece],
                 recv_sem=got.at[piece],
                 device_id=device,
                 device_id_type=MESH,
             ).start()
 
-        target[to, slot(xy_name), :] = source[at, slot(xy_name), :]
+        target[piece, slot(xy_name), :] = source[piece, slot(xy_name), :]
 
     def arrived(buffer, semaphore, piece):
         part = buffer.at[0, pl.ds(0, 480)]
         pltpu.make_async_copy(part, part, semaphore.at[piece]).wait()
 
-    def regroup(source, at, target, to):
+    def regroup(source, target, piece):
         for outer in range(16):
             for half in range(2):
-                target[to, pl.ds(outer * 32 + half * 16, 16), :] = source[
-                    at, pl.ds(half * 16 + outer, 16, stride=32), :
+                target[piece, pl.ds(outer * 32 + half * 16, 16), :] = source[
+                    piece, pl.ds(half * 16 + outer, 16, stride=32), :
                 ]
 
+    turn(0)
+    pl.semaphore_wait(barrier, 30)
     send_z(z_send, z_got, z_s, z_r, 0, True)
-    send_xy(xy_send, EARLY, early, 0, xy_s, xy_r, EARLY)
-    send_z(z_send, z_got, z_s, z_r, 1, True)
-    send_z(z_send, z_got, z_s, z_r, 3, True)
+    for piece in range(1, PIECES):
+        turn(piece)
+    send_xy(xy_send, xy_got, xy_s, xy_r, 1)
+    send_z(z_send, z_got, z_s, z_r, 2, True)
+    send_xy(xy_send, xy_got, xy_s, xy_r, 3)
 
     for copy in small:
         copy.wait()
     row, lane = iota((8, 128), 0), iota((8, 128), 1)
-    unmixed = z * 16384 + core * 16 + xy_name
+    unmixed = (z_name // 8) * 16384 + (z_name % 8) * 16 + xy_name
     place = jnp.where(
-        row < 3, (lane % 32) * 128, jnp.where(row < 6, (lane % 4) * 4096, unmixed + (lane % 4) * 32)
+        row < 3, (lane % 32) * 128, jnp.where(row < 6, (lane % 4) * 4096, unmixed + (lane % 4) * 32768)
     )
     phases = jnp.zeros((8, 128), F32)
     for layer in range(3):
@@ -311,74 +321,60 @@
         for k in range(64):
             mixed[piece, pl.ds(k * 8, 8), :] = tiles[k]
 
-    def inward(piece):
+    @pl.loop(0, PIECES, step=2)
+    def _(piece):
+        arrived(xy_got, xy_r, piece + 1)
+        regroup(xy_got, z_send, piece + 1)
+        send_z(z_send, z_got, z_s, z_r, piece + 1, True)
         arrived(z_got, z_r, piece)
-        regroup(z_got, piece, xy_send, piece)
-        send_xy(xy_send, piece, ready, piece, xy_s, xy_r, piece)
-
-    arrived(early, xy_r, EARLY)
-    regroup(early, 0, z_send, EARLY)
-    send_z(z_send, z_got, z_s, z_r, EARLY, True)
-
-    @pl.loop(0, 2)
-    def _(piece):
-        inward(piece)
+        regroup(z_got, xy_send, piece)
+        send_xy(xy_send, ready, xy_s, xy_r, piece)
 
     @pl.loop(0, PIECES)
     def _(piece):
-        @pl.when(piece == 1)
-        def _():
-            inward(3)
-
-        @pl.when(piece == EARLY)
-        def _():
-            arrived(z_got, z_r, EARLY)
-            regroup(z_got, EARLY, ready, EARLY)
-
-        @pl.when(piece != EARLY)
+        @pl.when(piece % 2 == 0)
         def _():
             arrived(ready, xy_r, piece)
 
+        @pl.when(piece % 2 == 1)
+        def _():
+            arrived(z_got, z_r, piece)
+            regroup(z_got, ready, piece)
+
         gates_on(piece)
 
-        @pl.when(piece < 2)
+        @pl.when(piece % 2 == 0)
         def _():
-            regroup(mixed, piece, z_back, piece)
+            regroup(mixed, z_back, piece)
             send_z(z_back, z_home, zb_s, zb_r, piece, False)
 
-        @pl.when(piece >= 2)
+        @pl.when(piece % 2 == 1)
         def _():
-            send_xy(mixed, piece, xy_home, piece, xyb_s, xyb_r, piece)
-
-    def finish_late(piece):
+            send_xy(mixed, xy_home, xyb_s, xyb_r, piece)
+
+    @pl.loop(0, PIECES, step=2)
+    def _(piece):
+        arrived(xy_home, xyb_r, piece + 1)
+        regroup(xy_home, z_back, piece + 1)
+        send_z(z_back, z_home, zb_s, zb_r, piece + 1, False)
         arrived(z_home, zb_r, piece)
-        regroup(z_home, piece, late, piece)
-        send_xy(late, piece, xy_home, piece, xyb_s, xyb_r, piece)
-
-    finish_late(0)
-
-    @pl.loop(2, PIECES)
-    def _(piece):
-        arrived(xy_home, xyb_r, piece)
-        regroup(xy_home, piece, z_back, piece)
-        send_z(z_back, z_home, zb_s, zb_r, piece, False)
-
-    finish_late(1)
-    for piece in range(2):
-        arrived(xy_home, xyb_r, piece)
-        arrived(z_home, zb_r, piece + 2)
-
-    @pl.loop(0, 16, unroll=16)
-    def _(block):
-        parts = []
-        for piece in range(PIECES):
-            for side in range(2):
-                name, half = (block // 2) * 2 + side, (block % 2) * 16
-                if piece < 2:
+        regroup(z_home, late, piece)
+        send_xy(late, xy_home, xyb_s, xyb_r, piece)
+
+    for piece in range(PIECES):
+        if piece % 2:
+            arrived(z_home, zb_r, piece)
+        else:
+            arrived(xy_home, xyb_r, piece)
+        for block in range(4):
+            parts = []
+            for part in range(8):
+                name, half = (block // 2) * 8 + part, (block % 2) * 16
+                if piece % 2:
+                    parts.append(z_home[piece, pl.ds(name * 32 + half, 16), :])
+                else:
                     parts.append(xy_home[piece, pl.ds(half + name, 16, stride=32), :])
-                else:
-                    parts.append(z_home[piece, pl.ds(pl.multiple_of(name * 32 + half, 16), 16), :])
-        out[pl.ds(pl.multiple_of(block * 128, 128), 128), :] = jnp.concatenate(parts, axis=0).T
+            out[pl.ds(piece * 512 + block * 128, 128), :] = jnp.concatenate(parts, axis=0).T
 
     for piece in range(PIECES):
         arrived(z_send, z_s, piece)
@@ -392,10 +388,7 @@
     linear = state.reshape(2, rows // 2, LANES).transpose(1, 0, 2).reshape(rows, LANES)
     hbm = pl.BlockSpec(memory_space=pltpu.HBM)
     whole = pltpu.VMEM((rows, LANES), F32)
-
-    def pieces(count):
-        return pltpu.VMEM((count, rows // PIECES, LANES), F32)
-
+    pieces = pltpu.VMEM((PIECES, rows // PIECES, LANES), F32)
     counts = pltpu.SemaphoreType.DMA((PIECES,))
     result = pl.pallas_call(
         kernel,
@@ -409,12 +402,11 @@
             pltpu.SMEM(coupled.shape, jnp.int32),
             pltpu.SMEM(sliced_index.shape, jnp.int32),
             pltpu.SMEM(sliced_values.shape, jnp.int32),
-            whole, pieces(4), pieces(4), pieces(4), pieces(1), pieces(4), pieces(4), pieces(2), pieces(4), pieces(4),
-            pieces(4),
+            whole, pieces, pieces, pieces, pieces, pieces, pieces, pieces, pieces, pieces, pieces,
             pltpu.VMEM((2, 256, 512), BF16),
             pltpu.VMEM((5, 2, 256, 256), BF16),
             pltpu.VMEM((PIECES, 2, 128, 256), BF16),
-            pltpu.SemaphoreType.DMA,
+            pltpu.SemaphoreType.DMA((4,)),
             pltpu.SemaphoreType.DMA((6,)),
             counts, counts, counts, counts, counts, counts, counts, counts,
         ],

time: 61.5 us -> 58.5 us (0.951)
  Pallas kernels: 60.4 us -> 57.4 us
    pallas_call x1, Pallas kernels: 60.4 us -> 57.4 us  [on_device(): pl.pallas_call(kernel, out_shape=pltpu.VMEM((rows, LANES), F32), in_specs...]
where the time goes in v3:
time: 58.5 us; the launch traced here: 58.4 us
  Pallas kernels  57.4 us (98%)
  local copies, waits for them, and re-layouts  0.97 us (2%)
    pallas_call x1, Pallas kernels, on_device(): pl.pallas_call(kernel, out_shape=pltpu.VMEM((rows, LANES), F32), in_specs...  57.4 us

profile of v3, /device:TPU:1, one launch (start us, length us, event | category | flops | bytes accessed | tf_op | source)
XLA Modules:
  0.0 58.4 jit_solution(10526614814272155201)
XLA Ops:
  0.0 57.4 %shard_map.73 = f32[2048,128]{1,0:T(8,128)S(1)} custom-call(f32[2048,128]{1,0:T(8,128)} %bitcast.11, f32[3,2,2,32,32]{4,3,2,1,0:T(8,128)} %gates_in.1, f32[3,2,2,32,32]{4,3,2,1,0:T(8,128)} %wide_in.1, f32[3,8]{1,0:T(4,128)} %angles_in.1, s32[3,8]{1,0:T(4,128)} %coupled_in.1, s32[3,8]{1,0:T(4,128)} %chosen_in.1, s32[14]{0:T(128)} %values_in.1), custom_call_target="tpu_custom_call" | custom-call | flops 2147483648 | bytes 2097152 | tf_op jit(solution)/shard_map/pallas_call | solution.py:393
  57.5 1.0 %copy.11 = f32[2,131072]{1,0:T(2,128)} copy(f32[2,131072]{1,0:T(2,128)S(1)} %bitcast.10) | data formatting | bytes 2097152

commit v4 on v3

--- a/solution.py
+++ b/solution.py
@@ -19,20 +19,24 @@
     return lax.broadcasted_iota(jnp.int32, shape, axis)
 
 
-def halves(value):
-    high = value.astype(BF16)
-    return high, (value - high.astype(F32)).astype(BF16)
-
-
-def thirds(value, axis):
+def split(value):
     high = value.astype(BF16)
     rest = value - high.astype(F32)
     middle = rest.astype(BF16)
-    return jnp.concatenate([high, middle, (rest - middle.astype(F32)).astype(BF16)], axis=axis)
+    return high, middle, (rest - middle.astype(F32)).astype(BF16)
+
+
+def thirds(value, axis):
+    return jnp.concatenate(split(value), axis=axis)
 
 
 def dot(left, right):
     return jnp.dot(left, right, preferred_element_type=F32)
+
+
+def six_products(left, right):
+    small = dot(left[0], right[2]) + dot(left[2], right[0]) + dot(left[1], right[1])
+    return dot(left[0], right[0]) + (dot(left[0], right[1]) + dot(left[1], right[0]) + small)
 
 
 def one_hot(wanted, own):
@@ -232,17 +236,19 @@
             plain = on_lanes(real, imag, wide_index, inner_index, wide_kept, inner_kept)
             times_i = on_lanes(-imag, real, wide_index, inner_index, wide_kept, inner_kept)
             first = jnp.dot(middle, jnp.concatenate([plain, times_i], axis=1), precision=HIGHEST, preferred_element_type=F32)
-            first_g[0], first_g[1] = halves(first)
+            first_g[0], first_g[1], first_g[2] = split(first)
         else:
             plain = on_lanes(real, imag, wide_index, wide_index, wide_kept, wide_kept)
             both = jnp.dot(middle, plain, precision=HIGHEST, preferred_element_type=F32)
-            rest_g[2 * layer - 1, 0], rest_g[2 * layer - 1, 1] = halves(both)
+            for part, value in enumerate(split(both)):
+                rest_g[2 * layer - 1, part] = value
         real, imag = wide[layer, 1, 0], wide[layer, 1, 1]
         if layer < 2:
             second = on_lanes(real, imag, wide_index, wide_index, wide_kept, wide_kept)
         else:
             second = on_lanes(real, imag, inner_index, wide_index, inner_kept, wide_kept)
-        rest_g[2 * layer, 0], rest_g[2 * layer, 1] = halves(second)
+        for part, value in enumerate(split(second)):
+            rest_g[2 * layer, part] = value
 
     top = [turned_gate(gates.at[:, 0], layer, layer + 3) for layer in range(3)]
     product = jnp.concatenate(top[0], axis=0)
@@ -269,19 +275,19 @@
         here = (row == 6) & (lane == piece)
         c = jnp.sum(jnp.where(here, cosine, 0.0))
         s = jnp.sum(jnp.where(here, sine, 0.0))
-        top_g[piece, 0], top_g[piece, 1] = halves(c * top_plain + s * top_times_i)
-
-    def right(tiles, zeros, ones, high, low_part):
+        for part, value in enumerate(split(c * top_plain + s * top_times_i)):
+            top_g[piece, part] = value
+
+    def right(tiles, zeros, ones, matrix):
         both = jnp.concatenate(
             [jnp.concatenate([tiles[k] for k in zeros], axis=0), jnp.concatenate([tiles[k] for k in ones], axis=0)], axis=1
         )
-        upper, lower = halves(both)
-        return dot(upper, high) + (dot(lower, high) + dot(upper, low_part))
+        return six_products(split(both), matrix)
 
     def gates_on(piece):
         tiles = [ready[piece, pl.ds(k * 8, 8), :] for k in range(64)]
         zeros = [k for k in range(64) if not k & 4]
-        product = right(tiles, zeros, [k | 4 for k in zeros], first_g[0], first_g[1])
+        product = right(tiles, zeros, [k | 4 for k in zeros], [first_g[part] for part in range(3)])
         found = {}
         for place, k in enumerate(zeros):
             for column in range(4):
@@ -303,9 +309,9 @@
                         axis=0,
                     )
                 )
-            upper, lower = halves(jnp.concatenate(columns, axis=1))
-            high, low_part = top_g[piece, 0], top_g[piece, 1]
-            topped = dot(high, upper) + (dot(low_part, upper) + dot(high, lower))
+            topped = six_products(
+                [top_g[piece, part] for part in range(3)], split(jnp.concatenate(columns, axis=1))
+            )
             for half in range(2):
                 for which, k in enumerate(groups[start + 4 * half : start + 4 * half + 4]):
                     for bit12 in range(2):
@@ -314,7 +320,7 @@
                             tiles[k | bit12 * 4 | bit13 * 2] = topped[at : at + 8, half * 128 : half * 128 + 128]
         for gate, mask in enumerate((8, 1, 16, 32, 4)):
             zeros = [k for k in range(64) if not k & mask]
-            product = right(tiles, zeros, [k | mask for k in zeros], rest_g[gate, 0], rest_g[gate, 1])
+            product = right(tiles, zeros, [k | mask for k in zeros], [rest_g[gate, part] for part in range(3)])
             for place, k in enumerate(zeros):
                 tiles[k] = product[place * 8 : place * 8 + 8, :128]
                 tiles[k | mask] = product[place * 8 : place * 8 + 8, 128:]
@@ -403,9 +409,9 @@
             pltpu.SMEM(sliced_index.shape, jnp.int32),
             pltpu.SMEM(sliced_values.shape, jnp.int32),
             whole, pieces, pieces, pieces, pieces, pieces, pieces, pieces, pieces, pieces, pieces,
-            pltpu.VMEM((2, 256, 512), BF16),
-            pltpu.VMEM((5, 2, 256, 256), BF16),
-            pltpu.VMEM((PIECES, 2, 128, 256), BF16),
+            pltpu.VMEM((3, 256, 512), BF16),
+            pltpu.VMEM((5, 3, 256, 256), BF16),
+            pltpu.VMEM((PIECES, 3, 128, 256), BF16),
             pltpu.SemaphoreType.DMA((4,)),
             pltpu.SemaphoreType.DMA((6,)),
             counts, counts, counts, counts, counts, counts, counts, counts,

time: 58.5 us -> 58.7 us (level)
  no operation moved by 1% of the time
where the time goes in v4:
time: 58.7 us; the launch traced here: 58.5 us
  Pallas kernels  57.5 us (98%)
  local copies, waits for them, and re-layouts  0.97 us (2%)
    pallas_call x1, Pallas kernels, on_device(): pl.pallas_call(kernel, out_shape=pltpu.VMEM((rows, LANES), F32), in_specs...  57.5 us

profile of v4, /device:TPU:1, one launch (start us, length us, event | category | flops | bytes accessed | tf_op | source)
XLA Modules:
  0.0 58.5 jit_solution(8932032115713367413)
XLA Ops:
  0.0 57.5 %shard_map.73 = f32[2048,128]{1,0:T(8,128)S(1)} custom-call(f32[2048,128]{1,0:T(8,128)} %bitcast.11, f32[3,2,2,32,32]{4,3,2,1,0:T(8,128)} %gates_in.1, f32[3,2,2,32,32]{4,3,2,1,0:T(8,128)} %wide_in.1, f32[3,8]{1,0:T(4,128)} %angles_in.1, s32[3,8]{1,0:T(4,128)} %coupled_in.1, s32[3,8]{1,0:T(4,128)} %chosen_in.1, s32[14]{0:T(128)} %values_in.1), custom_call_target="tpu_custom_call" | custom-call | flops 2147483648 | bytes 2097152 | tf_op jit(solution)/shard_map/pallas_call | solution.py:399
  57.5 1.0 %copy.11 = f32[2,131072]{1,0:T(2,128)} copy(f32[2,131072]{1,0:T(2,128)S(1)} %bitcast.10) | data formatting | bytes 2097152

commit v5 on v4

--- a/solution.py
+++ b/solution.py
@@ -99,13 +99,13 @@
 
     def z_peer(step):
         far = (step - 1) % 8
-        other = (z + 4 + (1 - 2 * (far % 2)) * ((far + 1) // 2)) % 8
-        side = (core + 1 + (step - 1) // 8) % 2
+        other = lax.rem(z + (4 + (1 - 2 * (far % 2)) * ((far + 1) // 2)), 8)
+        side = lax.rem(core + (1 + (step - 1) // 8), 2)
         lane = (other // 2) * 2 + side
-        return (x * 8 + (other % 2) * 4 + y, lane), other * 2 + side, (other % 2) * 8 + lane
+        return (x * 8 + lax.rem(other, 2) * 4 + y, lane), other * 2 + side, lax.rem(other, 2) * 8 + lane
 
     def xy_peer(step):
-        across, along = (x + step // 4) % 4, (y + step) % 4
+        across, along = lax.rem(x + step // 4, 4), lax.rem(y + step % 4, 4)
         return (across * 8 + low * 4 + along, n), across * 4 + along
 
     barrier = pltpu.get_barrier_semaphore()
@@ -119,12 +119,9 @@
     for load in loads:
         load.start()
 
-    @pl.loop(1, 16)
-    def _(step):
+    for step in range(1, 16):
         pl.semaphore_signal(barrier, inc=1, device_id=z_peer(step)[0], device_id_type=MESH)
-
-    @pl.loop(1, 16)
-    def _(step):
+    for step in range(1, 16):
         pl.semaphore_signal(barrier, inc=1, device_id=xy_peer(step)[0], device_id_type=MESH)
 
     small = [

time: 58.7 us -> 58.2 us (level)
  no operation moved by 1% of the time
where the time goes in v5:
time: 58.2 us; the launch traced here: 58.1 us
  Pallas kernels  57.1 us (98%)
  local copies, waits for them, and re-layouts  0.97 us (2%)
    pallas_call x1, Pallas kernels, on_device(): pl.pallas_call(kernel, out_shape=pltpu.VMEM((rows, LANES), F32), in_specs...  57.1 us

profile of v5, /device:TPU:1, one launch (start us, length us, event | category | flops | bytes accessed | tf_op | source)
XLA Modules:
  0.0 58.1 jit_solution(7293271805314601111)
XLA Ops:
  0.0 57.1 %shard_map.73 = f32[2048,128]{1,0:T(8,128)S(1)} custom-call(f32[2048,128]{1,0:T(8,128)} %bitcast.11, f32[3,2,2,32,32]{4,3,2,1,0:T(8,128)} %gates_in.1, f32[3,2,2,32,32]{4,3,2,1,0:T(8,128)} %wide_in.1, f32[3,8]{1,0:T(4,128)} %angles_in.1, s32[3,8]{1,0:T(4,128)} %coupled_in.1, s32[3,8]{1,0:T(4,128)} %chosen_in.1, s32[14]{0:T(128)} %values_in.1), custom_call_target="tpu_custom_call" | custom-call | flops 2147483648 | bytes 2097152 | tf_op jit(solution)/shard_map/pallas_call | solution.py:396
  57.1 1.0 %copy.11 = f32[2,131072]{1,0:T(2,128)} copy(f32[2,131072]{1,0:T(2,128)S(1)} %bitcast.10) | data formatting | bytes 2097152

commit v6 on v5

--- a/solution.py
+++ b/solution.py
@@ -153,8 +153,7 @@
 
 
     def send_z(source, target, sent, got, piece, inward):
-        @pl.loop(1, 16)
-        def _(step):
+        for step in range(1, 16):
             device, name, there = z_peer(step)
             pltpu.make_async_remote_copy(
                 src_ref=source.at[piece, slot(name if inward else there)],
@@ -169,8 +168,7 @@
         target[piece, slot(landing), :] = source[piece, slot(own), :]
 
     def send_xy(source, target, sent, got, piece):
-        @pl.loop(1, 16)
-        def _(step):
+        for step in range(1, 16):
             device, name = xy_peer(step)
             pltpu.make_async_remote_copy(
                 src_ref=source.at[piece, slot(name)],

time: 58.2 us -> 58.2 us (level)
  no operation moved by 1% of the time
where the time goes in v6:
time: 58.2 us; the launch traced here: 58.1 us
  Pallas kernels  57.1 us (98%)
  local copies, waits for them, and re-layouts  0.97 us (2%)
    pallas_call x1, Pallas kernels, on_device(): pl.pallas_call(kernel, out_shape=pltpu.VMEM((rows, LANES), F32), in_specs...  57.1 us

profile of v6, /device:TPU:1, one launch (start us, length us, event | category | flops | bytes accessed | tf_op | source)
XLA Modules:
  0.0 58.1 jit_solution(6336406808201673673)
XLA Ops:
  0.0 57.1 %shard_map.73 = f32[2048,128]{1,0:T(8,128)S(1)} custom-call(f32[2048,128]{1,0:T(8,128)} %bitcast.11, f32[3,2,2,32,32]{4,3,2,1,0:T(8,128)} %gates_in.1, f32[3,2,2,32,32]{4,3,2,1,0:T(8,128)} %wide_in.1, f32[3,8]{1,0:T(4,128)} %angles_in.1, s32[3,8]{1,0:T(4,128)} %coupled_in.1, s32[3,8]{1,0:T(4,128)} %chosen_in.1, s32[14]{0:T(128)} %values_in.1), custom_call_target="tpu_custom_call" | custom-call | flops 2147483648 | bytes 2097152 | tf_op jit(solution)/shard_map/pallas_call | solution.py:394
  57.1 1.0 %copy.11 = f32[2,131072]{1,0:T(2,128)} copy(f32[2,131072]{1,0:T(2,128)S(1)} %bitcast.10) | data formatting | bytes 2097152
